TPU v7x, 512 devices: a whole 4x4x16 slice. The times are simulated.
512 devices in a mesh: face: 4 (over z_lo), tile: 64 (over y, z_hi, x), lev: 2 (over core).
Axes of the slice: x: 4, y: 4, z: 16 (z_hi: 4, z_lo: 4; z = z_hi * 4 + z_lo), core: 2. Of those that a mesh axis runs over, the one named last changes fastest.
Arguments:
- flux: float32 [2048, 8, 512], P(('face', 'tile')), may hold values from -6 to 6
- profile: float32 [16], P('lev'), may hold values from 0.2 to 1
- courant: float32 [2, 16, 512, 2048], P(None, 'lev', 'tile', 'face'), may hold values from 0.05 to 0.45
- winds: int32 [2, 16, 512, 2048], P(None, 'lev', 'tile', 'face'), may hold values from 0 to 1
- cells: int32 [64, 4, 128], P('tile', 'face'), may hold values from 0 to 4095, as said below
- counts: int32 [64, 4], P('tile', 'face'), may hold values from 32 to 128, as said below
- kernels: float32 [16, 64, 4, 128], P('lev', 'tile', 'face'), may hold values from 0.25 to 0.75
- month_weight: float32 [8, 64, 4, 128], P(None, 'tile', 'face'), may hold values from 0 to 1
- observed: float32 [64, 4, 128], P('tile', 'face'), may hold values from -8 to 8
- obs_weight: float32 [64, 4, 128], P('tile', 'face'), may hold values from 0.5 to 2
- precision: float32 [8], replicated, may hold values from 0.5 to 2
Outputs:
- flux_gradient: float32 [8, 512, 2048], P(None, 'tile', 'face')
- precision_gradient: float32 [8], replicated
Inputs may be any that keep to these rules, and one draw needn't show every extreme that they name: Within each block the 128 entries are distinct cells, numbered row by row over the block's 8 rows of 512 cells; the first four slots of every block hold, in some order, a cell of the block's first column, one of its last column, and interior cells of its first row and of its last row. `counts`: slot s of a block holds a sounding when s is below the block's count; some block is full and some holds exactly 32.
All inputs are finite; a program needn't handle non-finite values.
Results may differ from a plain program's by a relative error of at most 0.00015.
Values sent between devices are 32-bit elements; how exact they have to be, the bound alone decides.
A program may use at most 64 MiB of HBM per device.

v0:
```python
import jax
import jax.numpy as jnp
from jax import lax
from jax.sharding import PartitionSpec as P

KAPPA = 0.025


def extended(x, sides, width, wrap):
    for axis, dim in sides:
        devices, length = (lax.axis_size(axis), x.shape[dim])
        up = [(i, (i + 1) % devices) for i in range(devices if wrap else devices - 1)]
        down = [(j, i) for i, j in up]
        last = lax.slice_in_dim(x, length - width, length, axis=dim)
        initial = lax.slice_in_dim(x, 0, width, axis=dim)
        before = lax.ppermute(last, axis, up)
        after = lax.ppermute(initial, axis, down)
        x = jnp.concatenate([before, x, after], axis=dim)
    return x


def shifted(x, axis, by):
    devices = lax.axis_size(axis)
    return lax.ppermute(x, axis, [(i, (i + by) % devices) for i in range(devices)])


def shifted_2(value, axis, steps):
    count = lax.axis_size(axis)
    initial, last = (max(0, -steps), min(count, count - steps))
    return lax.ppermute(value, axis, [(source, source + steps) for source in range(initial, last)])


def weights_from(speed_x, speed_y, east_flag, north_flag):
    w_west = speed_x * (1.0 - east_flag) + KAPPA
    w_east = speed_x * east_flag + KAPPA
    w_south = speed_y * (1.0 - north_flag) + KAPPA
    w_north = speed_y * north_flag + KAPPA
    w_centre = 1.0 - speed_x - speed_y - 4.0 * KAPPA
    return (w_centre, w_west, w_east, w_south, w_north)


def flags_of(winds):
    return ((winds[0] == 1).astype(jnp.float32), (winds[1] == 1).astype(jnp.float32))


def advance(conc, coeffs):
    w_centre, w_west, w_east, w_south, w_north = coeffs
    side = extended(conc, (("face", 3),), 1, True)
    rim = extended(conc, (("tile", 2),), 1, False)
    return (
        w_centre * conc
        + w_west * side[..., :-2]
        + w_east * side[..., 2:]
        + w_south * rim[..., :-2, :]
        + w_north * rim[..., 2:, :]
    )


def retreat(grad, coeffs):
    w_centre, w_west, w_east, w_south, w_north = coeffs
    west_weighted = w_west * grad
    east_weighted = w_east * grad
    south_weighted = w_south * grad
    north_weighted = w_north * grad
    from_east = shifted(west_weighted[..., :1], "face", -1)
    from_west = shifted(east_weighted[..., -1:], "face", 1)
    from_above = shifted_2(south_weighted[..., :1, :], "tile", -1)
    from_below = shifted_2(north_weighted[..., -1:, :], "tile", 1)
    west_part = jnp.concatenate([west_weighted[..., 1:], from_east], -1)
    east_part = jnp.concatenate([from_west, east_weighted[..., :-1]], -1)
    south_part = jnp.concatenate([south_weighted[..., 1:, :], from_above], -2)
    north_part = jnp.concatenate([from_below, north_weighted[..., :-1, :]], -2)
    return w_centre * grad + west_part + east_part + south_part + north_part


def on_device(
    flux,
    profile,
    courant,
    winds,
    cells,
    counts,
    kernels,
    month_weight,
    observed,
    obs_weight,
    precision,
):
    n_tracer = flux.shape[1]
    n_level = profile.shape[0]
    slot_total = cells.shape[2]
    moved = lax.all_to_all(flux, "tile", split_axis=2, concat_axis=0, tiled=True)
    field = jnp.transpose(moved, (1, 2, 0))
    rows_dev = field.shape[1]
    cols_dev = field.shape[2]
    n_cell = rows_dev * cols_dev
    east_flag, north_flag = flags_of(winds)
    conc = profile[None, :, None, None] * field[:, None]
    coeffs = weights_from(courant[0], courant[1], east_flag, north_flag)
    conc = advance(advance(conc, coeffs), coeffs)
    slot_cells = cells.reshape(slot_total)
    live = jnp.arange(slot_total, dtype=jnp.int32) < counts.reshape(())
    picker = jnp.where(
        live[:, None] & (slot_cells[:, None] == jnp.arange(n_cell, dtype=jnp.int32)[None, :]),
        1.0,
        0.0,
    ).astype(jnp.float32)
    flat = conc.reshape(n_tracer, n_level, n_cell)
    sampled = jnp.einsum("tlc,sc->tls", flat, picker, precision=lax.Precision.HIGHEST)
    kern = kernels.reshape(n_level, slot_total)
    monthly = month_weight.reshape(n_tracer, slot_total)
    partial_model = jnp.sum(kern * jnp.sum(monthly[:, None, :] * sampled, 0), 0)
    model = lax.psum(partial_model, "lev")
    forcing = jnp.where(
        live, obs_weight.reshape(slot_total) * (observed.reshape(slot_total) - model), 0.0
    )
    values = kern[None] * (monthly * forcing[None])[:, None, :]
    lam = jnp.einsum("tls,sc->tlc", values, picker, precision=lax.Precision.HIGHEST)
    lam = lam.reshape(n_tracer, n_level, rows_dev, cols_dev)
    lam = retreat(retreat(lam, coeffs), coeffs)
    adj_part = jnp.sum(profile[None, :, None, None] * lam, 1)
    all_cells = n_cell * lax.axis_size("tile") * lax.axis_size("face")
    adj = lax.psum(adj_part, "lev")
    flux_gradient = precision[:, None, None] * field - adj
    square_sum = lax.psum(jnp.sum(adj * adj, axis=(1, 2)), ("face", "tile"))
    precision_gradient = 0.5 / precision - 0.5 * (square_sum / all_cells) / (precision * precision)
    return (flux_gradient, precision_gradient)


def solution(mesh):
    return jax.shard_map(
        on_device,
        mesh=mesh,
        in_specs=(
            P(("face", "tile"), None, None),
            P("lev"),
            P(None, "lev", "tile", "face"),
            P(None, "lev", "tile", "face"),
            P("tile", "face", None),
            P("tile", "face"),
            P("lev", "tile", "face", None),
            P(None, "tile", "face", None),
            P("tile", "face", None),
            P("tile", "face", None),
            P(),
        ),
        out_specs=(P(None, "tile", "face"), P()),
        check_vma=False,
    )
```

profile of v0, /device:TPU:32, one launch (start us, length us, event | category | flops | bytes accessed | tf_op | source)
XLA Modules:
  0.0 1168.7 jit_solution(5610475102505204907)
XLA Ops:
  7.2 1.7 copy.25
  8.9 1.7 reshape.69
  10.6 20.3 %all-to-all-start = ((f32[64,1,512]{2,1,0:T(1,128)}), f32[64,1,512]{2,1,0:T(1,128)S(1)}, u32[]{:S(2)}, u32[]{:S(2)}) async-start(f32[64,1,512]{2,1,0:T(1,128)} %reshape.69), calls=%async_computation | async-start | bytes 262144 | tf_op jit(solution)/shard_map/all_to_all | solution.py:92
  31.1 20.0 %all-to-all-done = f32[64,1,512]{2,1,0:T(1,128)S(1)} async-done(((f32[64,1,512]{2,1,0:T(1,128)}), f32[64,1,512]{2,1,0:T(1,128)S(1)}, u32[]{:S(2)}, u32[]{:S(2)}) %all-to-all-start) | async-done | bytes 131104 | tf_op jit(solution)/shard_map/all_to_all | solution.py:92
  51.1 0.5 broadcast.82
  51.6 0.9 reduce.1
  52.6 1.1 reshape.70
  53.7 2.4 copy.27
  56.1 2.8 all_to_all.16
  58.9 0.2 broadcast_multiply_fusion.8
  59.1 0.1 fusion.52
  59.3 2.5 collective-permute-start.2
  61.8 1.3 collective-permute-start.3
  63.1 2.9 collective-permute-start
  66.1 2.9 collective-permute-start.1
  69.7 0.1 copy.31
  69.8 0.1 copy.29
  69.9 0.1 copy.30
  70.0 0.1 copy.32
  70.0 0.1 copy.28
  70.1 4.1 collective-permute-done
  74.2 7.7 collective-permute-done.1
  81.9 0.8 fusion.24
  82.7 1.3 collective-permute-start.6
  84.0 1.3 collective-permute-start.7
  85.3 0.1 fusion.50
  85.5 5.5 collective-permute-start.4
  91.0 1.9 collective-permute-start.5
  93.0 7.6 collective-permute-done.4
  100.5 0.8 fusion.16
  101.3 2.4 fusion.12
  103.8 2.6 psum.21
  106.5 1.7 fusion
  108.2 0.6 broadcast_multiply_fusion.5
  108.8 1.3 collective-permute-start.10
  110.1 4.9 collective-permute-start.11
  115.1 0.1 slice.162
  115.2 3.2 collective-permute-start.8
  118.4 3.1 collective-permute-start.9
  121.6 0.1 copy.35
  121.7 0.1 slice.167
  121.7 0.1 slice.164
  121.8 0.3 slice.160
  122.2 3.8 collective-permute-done.8
  126.0 6.6 collective-permute-done.9
  132.5 1.1 broadcast_multiply_fusion.6
  133.6 4.2 collective-permute-start.12
  137.9 0.2 broadcast_multiply_fusion.4
  138.1 0.3 slice.168
  138.6 5.9 collective-permute-start.15
  144.5 1.3 collective-permute-start.14
  145.8 0.1 slice.170
  146.0 3.7 collective-permute-start.13
  149.7 0.2 pad_maximum_fusion.12
  149.8 7.5 collective-permute-done.13
  157.3 0.3 pad_maximum_fusion.13
  157.7 0.1 pad_maximum_fusion.15
  157.8 9.1 collective-permute-done.14
  167.0 1.1 multiply_reduce_fusion
  168.1 0.7 copy.38
  168.8 66.5 %all-reduce.2.cloned.1.call-done = f32[8,8,512]{2,1,0:T(8,128)} async-done(((f32[8,8,512]{2,1,0:T(8,128)}), f32[8,8,512]{2,1,0:T(8,128)}) %all-reduce.2.cloned.1.call-update) | async-done | bytes 131088 | tf_op jit(solution)/shard_map/psum | solution.py:123
  235.3 1.7 multiply_reduce_fusion.1
  237.0 924.4 %psum.23 = f32[8]{0:T(128)S(1)} all-reduce(f32[8]{0:T(128)S(1)} %get-tuple-element.33), channel_id=1, replica_groups=mesh['face'=4,'tile'=64,'lev'=2] {'face','tile'}, use_global_device_ids=true, to_apply=%region_6.7 | all-reduce | flops 8 | bytes 64 | tf_op jit(solution)/shard_map/psum | solution.py:125
  1161.3 0.5 divide_subtract_fusion
  (46 shorter events, 0.6 us)
Async XLA Ops:
  7.2 23.8 %copy-start = (f32[2,8,8,512]{3,2,1,0:T(8,128)S(1)}, f32[2,8,8,512]{3,2,1,0:T(8,128)}, u32[]{:S(2)}) copy-start(f32[2,8,8,512]{3,2,1,0:T(8,128)} %param.13) | copy-start | bytes 786436
  7.2 23.8 %copy-start.1 = (s32[2,8,8,512]{3,2,1,0:T(8,128)S(1)}, s32[2,8,8,512]{3,2,1,0:T(8,128)}, u32[]{:S(2)}) copy-start(s32[2,8,8,512]{3,2,1,0:T(8,128)} %param.14) | copy-start | bytes 786436
  10.6 40.5 %all-to-all-start = ((f32[64,1,512]{2,1,0:T(1,128)}), f32[64,1,512]{2,1,0:T(1,128)S(1)}, u32[]{:S(2)}, u32[]{:S(2)}) async-start(f32[64,1,512]{2,1,0:T(1,128)} %reshape.69), calls=%async_computation | async-start | bytes 262144 | tf_op jit(solution)/shard_map/all_to_all | solution.py:92
  30.9 204.3 %all-reduce.2.cloned.1.call-start = ((), (), s32[]{:S(2)}) async-start(), calls=%async_computation.1 | async-start | bytes 262144 | tf_op jit(solution)/shard_map/psum | solution.py:123
  56.1 2.8 copy-start.4
  59.3 22.6 %collective-permute-start.2 = (f32[8,8,1,512]{3,1,2,0:T(8,128)S(1)}, f32[8,8,1,512]{3,1,2,0:T(8,128)S(1)}, u32[]{:S(2)}, u32[]{:S(2)}) collective-permute-start(f32[8,8,1,512]{3,1,2,0:T(8,128)S(1)} %get-tuple-element.25), channel_id=1, source_target_pairs={{0,2},{2,4},{4,6},{6,8},{8,10},{10,12},{12,14},{14,16},{16,18},{18... | collective-permute-start | bytes 393224 | tf_op jit(solution)/shard_map/ppermute | solution.py:16
  61.8 20.1 %collective-permute-start.3 = (f32[8,8,1,512]{3,1,2,0:T(8,128)S(1)}, f32[8,8,1,512]{3,1,2,0:T(8,128)S(1)}, u32[]{:S(2)}, u32[]{:S(2)}) collective-permute-start(f32[8,8,1,512]{3,1,2,0:T(8,128)S(1)} %get-tuple-element.26), channel_id=1, source_target_pairs={{2,0},{4,2},{6,4},{8,6},{10,8},{12,10},{14,12},{16,14},{18,16},{20... | collective-permute-start | bytes 393224 | tf_op jit(solution)/shard_map/ppermute | solution.py:17
  63.1 11.1 collective-permute-start
  66.1 15.9 %collective-permute-start.1 = (f32[8,8,8,1]{3,1,2,0:T(8,128)S(1)}, f32[8,8,8,1]{3,1,2,0:T(8,128)S(1)}, u32[]{:S(2)}, u32[]{:S(2)}) collective-permute-start(f32[8,8,8,1]{3,1,2,0:T(8,128)S(1)} %get-tuple-element.24), channel_id=1, source_target_pairs={{128,0},{256,128},{384,256},{0,384},{129,1},{257,129},{385,257},{1... | collective-permute-start | bytes 6152 | tf_op jit(solution)/shard_map/ppermute | solution.py:17
  82.7 17.8 %collective-permute-start.6 = (f32[8,8,1,512]{3,1,2,0:T(8,128)S(1)}, f32[8,8,1,512]{3,1,2,0:T(8,128)S(1)}, u32[]{:S(2)}, u32[]{:S(2)}) collective-permute-start(f32[8,8,1,512]{3,1,2,0:T(8,128)S(1)} %get-tuple-element.21), channel_id=1, source_target_pairs={{0,2},{2,4},{4,6},{6,8},{8,10},{10,12},{12,14},{14,16},{16,18},{18... | collective-permute-start | bytes 393224 | tf_op jit(solution)/shard_map/ppermute | solution.py:16
  84.0 17.3 %copy-start.2 = (f32[8,1,1,128]{3,2,1,0:T(1,128)S(1)}, f32[8,1,1,128]{3,2,1,0:T(1,128)}, u32[]{:S(2)}) copy-start(f32[8,1,1,128]{3,2,1,0:T(1,128)} %param.18) | copy-start | bytes 12292
  84.0 17.3 %copy-start.8 = (s32[1,1,128]{2,1,0:T(1,128)S(1)}, s32[1,1,128]{2,1,0:T(1,128)}, u32[]{:S(2)}) copy-start(s32[1,1,128]{2,1,0:T(1,128)} %param.15) | copy-start | bytes 1540
  84.0 16.5 %collective-permute-start.7 = (f32[8,8,1,512]{3,1,2,0:T(8,128)S(1)}, f32[8,8,1,512]{3,1,2,0:T(8,128)S(1)}, u32[]{:S(2)}, u32[]{:S(2)}) collective-permute-start(f32[8,8,1,512]{3,1,2,0:T(8,128)S(1)} %get-tuple-element.22), channel_id=1, source_target_pairs={{2,0},{4,2},{6,4},{8,6},{10,8},{12,10},{14,12},{16,14},{18,16},{20... | collective-permute-start | bytes 393224 | tf_op jit(solution)/shard_map/ppermute | solution.py:17
  85.5 15.0 %collective-permute-start.4 = (f32[8,8,8,1]{3,1,2,0:T(8,128)S(1)}, f32[8,8,8,1]{3,1,2,0:T(8,128)S(1)}, u32[]{:S(2)}, u32[]{:S(2)}) collective-permute-start(f32[8,8,8,1]{3,1,2,0:T(8,128)S(1)} %get-tuple-element.19), channel_id=1, source_target_pairs={{0,128},{128,256},{256,384},{384,0},{1,129},{129,257},{257,385},{3... | collective-permute-start | bytes 6152 | tf_op jit(solution)/shard_map/ppermute | solution.py:16
  91.0 9.6 collective-permute-start.5
  92.9 10.9 copy-start.3
  92.9 13.5 %copy-start.6 = (f32[1,1,128]{2,1,0:T(1,128)S(1)}, f32[1,1,128]{2,1,0:T(1,128)}, u32[]{:S(2)}) copy-start(f32[1,1,128]{2,1,0:T(1,128)} %param.19) | copy-start | bytes 1540
  92.9 13.5 %copy-start.7 = (f32[1,1,128]{2,1,0:T(1,128)S(1)}, f32[1,1,128]{2,1,0:T(1,128)}, u32[]{:S(2)}) copy-start(f32[1,1,128]{2,1,0:T(1,128)} %param.20) | copy-start | bytes 1540
  108.8 23.7 %collective-permute-start.10 = (f32[8,8,1,512]{3,1,2,0:T(8,128)S(1)}, f32[8,8,1,512]{3,1,2,0:T(8,128)S(1)}, u32[]{:S(2)}, u32[]{:S(2)}) collective-permute-start(f32[8,8,1,512]{3,1,2,0:T(8,128)S(1)} %slice.165), channel_id=1, source_target_pairs={{2,0},{4,2},{6,4},{8,6},{10,8},{12,10},{14,12},{16,14},{18,16},{20... | collective-permute-start | bytes 393224 | tf_op jit(solution)/shard_map/ppermute | solution.py:30
  110.1 22.4 %collective-permute-start.11 = (f32[8,8,1,512]{3,1,2,0:T(8,128)S(1)}, f32[8,8,1,512]{3,1,2,0:T(8,128)S(1)}, u32[]{:S(2)}, u32[]{:S(2)}) collective-permute-start(f32[8,8,1,512]{3,1,2,0:T(8,128)S(1)} %slice.166), channel_id=1, source_target_pairs={{0,2},{2,4},{4,6},{6,8},{8,10},{10,12},{12,14},{14,16},{16,18},{18... | collective-permute-start | bytes 393224 | tf_op jit(solution)/shard_map/ppermute | solution.py:30
  115.2 10.7 collective-permute-start.8
  118.4 14.1 %collective-permute-start.9 = (f32[8,8,8,1]{3,1,2,0:T(8,128)S(1)}, f32[8,8,8,1]{3,1,2,0:T(8,128)S(1)}, u32[]{:S(2)}, u32[]{:S(2)}) collective-permute-start(f32[8,8,8,1]{3,1,2,0:T(8,128)S(1)} %slice.162), channel_id=1, source_target_pairs={{0,128},{128,256},{256,384},{384,0},{1,129},{129,257},{257,385},{3... | collective-permute-start | bytes 6152 | tf_op jit(solution)/shard_map/ppermute | solution.py:24
  133.6 16.0 %collective-permute-start.12 = (f32[8,8,8,1]{3,1,2,0:T(8,128)S(1)}, f32[8,8,8,1]{3,1,2,0:T(8,128)S(1)}, u32[]{:S(2)}, u32[]{:S(2)}) collective-permute-start(f32[8,8,8,1]{3,1,2,0:T(8,128)S(1)} %slice.169), channel_id=1, source_target_pairs={{0,384},{128,0},{256,128},{384,256},{1,385},{129,1},{257,129},{385... | collective-permute-start | bytes 6152 | tf_op jit(solution)/shard_map/ppermute | solution.py:24
  138.6 19.1 %collective-permute-start.15 = (f32[8,8,1,512]{3,1,2,0:T(8,128)S(1)}, f32[8,8,1,512]{3,1,2,0:T(8,128)S(1)}, u32[]{:S(2)}, u32[]{:S(2)}) collective-permute-start(f32[8,8,1,512]{3,1,2,0:T(8,128)S(1)} %slice.174), channel_id=1, source_target_pairs={{0,2},{2,4},{4,6},{6,8},{8,10},{10,12},{12,14},{14,16},{16,18},{18... | collective-permute-start | bytes 393224 | tf_op jit(solution)/shard_map/ppermute | solution.py:30
  144.5 22.3 %collective-permute-start.14 = (f32[8,8,1,512]{3,1,2,0:T(8,128)S(1)}, f32[8,8,1,512]{3,1,2,0:T(8,128)S(1)}, u32[]{:S(2)}, u32[]{:S(2)}) collective-permute-start(f32[8,8,1,512]{3,1,2,0:T(8,128)S(1)} %slice.173), channel_id=1, source_target_pairs={{2,0},{4,2},{6,4},{8,6},{10,8},{12,10},{14,12},{16,14},{18,16},{20... | collective-permute-start | bytes 393224 | tf_op jit(solution)/shard_map/ppermute | solution.py:30
  146.0 11.4 collective-permute-start.13
  166.9 68.3 %copy-start.5 = (f32[8]{0:T(128)S(1)}, f32[8]{0:T(128)}, u32[]{:S(2)}) copy-start(f32[8]{0:T(128)} %param.21) | copy-start | bytes 100
Sparse Core Ops, SparseCore 0:
  169.0 66.2 all-reduce.1
where the time goes:
time: 1170 us
  blocking collectives  927 us (79%)
  waiting for transfers between devices  133 us (11%)
  starting transfers between devices  67.6 us (6%)
  between operations  15.2 us (1%)
  local copies, waits for them, and re-layouts  13.2 us (1%)
    psum x1, blocking collectives, on_device(): square_sum = lax.psum(jnp.sum(adj * adj, axis=(1, 2)), ('face', 'tile'))  924 us
    psum x1, waiting for transfers between devices, on_device(): adj = lax.psum(adj_part, 'lev')  66.5 us
  transfers between devices with their start and end apart: 18, of which 9 were waited for; matrix products, arithmetic and copies ran while one was open for 0% of the time, Pallas kernels for 0%

commit v1 on v0

--- a/solution.py
+++ b/solution.py
@@ -2,6 +2,7 @@
 import jax.numpy as jnp
 from jax import lax
 from jax.sharding import PartitionSpec as P
+from jax.lax import psum
 
 KAPPA = 0.025
 
@@ -122,7 +123,9 @@
     all_cells = n_cell * lax.axis_size("tile") * lax.axis_size("face")
     adj = lax.psum(adj_part, "lev")
     flux_gradient = precision[:, None, None] * field - adj
-    square_sum = lax.psum(jnp.sum(adj * adj, axis=(1, 2)), ("face", "tile"))
+    square_sum = jnp.sum(adj * adj, axis=(1, 2))
+    for d in ("face", "tile"):
+        square_sum = psum(square_sum, d)
     precision_gradient = 0.5 / precision - 0.5 * (square_sum / all_cells) / (precision * precision)
     return (flux_gradient, precision_gradient)
 

time: 1170 us -> 480 us (0.41)
  blocking collectives: 927 us -> 237 us
    psum x1 -> x2, blocking collectives: 924 us -> 235 us  [on_device(): square_sum = psum(square_sum, d)]
  transfers between devices with their start and end apart: 18 -> 18, of which waited for: 9 -> 9; matrix products, arithmetic and copies ran while one was open for 0% -> 1% of each run, Pallas kernels for 0% -> 0%
where the time goes in v1:
time: 480 us; the launch traced here: 479 us
  blocking collectives  237 us (49%)
  waiting for transfers between devices  133 us (28%)
  starting transfers between devices  67.6 us (14%)
  between operations  15.2 us (3%)
  local copies, waits for them, and re-layouts  13.2 us (3%)
  other arithmetic  8.64 us (2%)
    psum x2, blocking collectives, on_device(): square_sum = psum(square_sum, d)  235 us
    psum x1, waiting for transfers between devices, on_device(): adj = lax.psum(adj_part, 'lev')  66.4 us
    all_to_all x1, starting transfers between devices, on_device(): lax.all_to_all(flux, 'tile', split_axis=2, concat_axis=0, tiled=True)  20.3 us
    all_to_all x1, waiting for transfers between devices, on_device(): lax.all_to_all(flux, 'tile', split_axis=2, concat_axis=0, tiled=True)  20 us
    ppermute x4, waiting for transfers between devices, shifted(): lax.ppermute(x, axis, [(i, (i + by) % devices) for i in range(devices)])  17.9 us
    ppermute x4, starting transfers between devices, shifted(): lax.ppermute(x, axis, [(i, (i + by) % devices) for i in range(devices)])  14.3 us
    ppermute x4, starting transfers between devices, shifted_2(): lax.ppermute(value, axis, [(source, source + steps) for source in range(i...  13.4 us
    ppermute x4, starting transfers between devices, extended(): before = lax.ppermute(last, axis, up)  12.2 us
  transfers between devices with their start and end apart: 18, of which 9 were waited for; matrix products, arithmetic and copies ran while one was open for 1% of the time, Pallas kernels for 0%

profile of v1, /device:TPU:32, one launch (start us, length us, event | category | flops | bytes accessed | tf_op | source)
XLA Modules:
  0.0 478.9 jit_solution(14641408444181761715)
XLA Ops:
  7.2 1.7 copy.25
  8.9 1.7 reshape.69
  10.6 20.3 %all-to-all-start = ((f32[64,1,512]{2,1,0:T(1,128)}), f32[64,1,512]{2,1,0:T(1,128)S(1)}, u32[]{:S(2)}, u32[]{:S(2)}) async-start(f32[64,1,512]{2,1,0:T(1,128)} %reshape.69), calls=%async_computation | async-start | bytes 262144 | tf_op jit(solution)/shard_map/all_to_all | solution.py:93
  31.1 20.0 %all-to-all-done = f32[64,1,512]{2,1,0:T(1,128)S(1)} async-done(((f32[64,1,512]{2,1,0:T(1,128)}), f32[64,1,512]{2,1,0:T(1,128)S(1)}, u32[]{:S(2)}, u32[]{:S(2)}) %all-to-all-start) | async-done | bytes 131104 | tf_op jit(solution)/shard_map/all_to_all | solution.py:93
  51.1 0.5 broadcast.82
  51.6 0.9 reduce.1
  52.6 1.1 reshape.70
  53.7 2.4 copy.27
  56.1 2.8 all_to_all.16
  58.9 0.2 broadcast_multiply_fusion.8
  59.1 0.1 fusion.52
  59.3 2.5 collective-permute-start.2
  61.8 1.3 collective-permute-start.3
  63.1 2.9 collective-permute-start
  66.1 2.9 collective-permute-start.1
  69.7 0.1 copy.31
  69.8 0.1 copy.29
  69.9 0.1 copy.30
  69.9 0.1 copy.32
  70.0 0.1 copy.28
  70.1 4.1 collective-permute-done
  74.2 7.7 %collective-permute-done.1 = f32[8,8,8,1]{3,1,2,0:T(8,128)S(1)} collective-permute-done((f32[8,8,8,1]{3,1,2,0:T(8,128)S(1)}, f32[8,8,8,1]{3,1,2,0:T(8,128)S(1)}, u32[]{:S(2)}, u32[]{:S(2)}) %collective-permute-start.1) | collective-permute-done | bytes 2080 | tf_op jit(solution)/shard_map/ppermute | solution.py:18
  81.9 0.8 fusion.24
  82.7 1.3 collective-permute-start.6
  84.0 1.3 collective-permute-start.7
  85.3 0.1 fusion.50
  85.5 5.5 %collective-permute-start.4 = (f32[8,8,8,1]{3,1,2,0:T(8,128)S(1)}, f32[8,8,8,1]{3,1,2,0:T(8,128)S(1)}, u32[]{:S(2)}, u32[]{:S(2)}) collective-permute-start(f32[8,8,8,1]{3,1,2,0:T(8,128)S(1)} %get-tuple-element.19), channel_id=1, source_target_pairs={{0,128},{128,256},{256,384},{384,0},{1,129},{129,257},{257,385},{3... | collective-permute-start | bytes 6152 | tf_op jit(solution)/shard_map/ppermute | solution.py:17
  91.0 1.9 collective-permute-start.5
  93.0 7.6 %collective-permute-done.4 = f32[8,8,8,1]{3,1,2,0:T(8,128)S(1)} collective-permute-done((f32[8,8,8,1]{3,1,2,0:T(8,128)S(1)}, f32[8,8,8,1]{3,1,2,0:T(8,128)S(1)}, u32[]{:S(2)}, u32[]{:S(2)}) %collective-permute-start.4) | collective-permute-done | bytes 2080 | tf_op jit(solution)/shard_map/ppermute | solution.py:17
  100.5 0.8 fusion.16
  101.3 2.5 fusion.12
  103.8 2.6 psum.28
  106.5 1.7 fusion
  108.2 0.6 broadcast_multiply_fusion.5
  108.8 1.3 collective-permute-start.10
  110.1 4.9 %collective-permute-start.11 = (f32[8,8,1,512]{3,1,2,0:T(8,128)S(1)}, f32[8,8,1,512]{3,1,2,0:T(8,128)S(1)}, u32[]{:S(2)}, u32[]{:S(2)}) collective-permute-start(f32[8,8,1,512]{3,1,2,0:T(8,128)S(1)} %slice.166), channel_id=1, source_target_pairs={{0,2},{2,4},{4,6},{6,8},{8,10},{10,12},{12,14},{14,16},{16,18},{18... | collective-permute-start | bytes 393224 | tf_op jit(solution)/shard_map/ppermute | solution.py:31
  115.0 0.1 slice.162
  115.2 3.2 collective-permute-start.8
  118.4 3.1 collective-permute-start.9
  121.6 0.1 copy.35
  121.7 0.1 slice.164
  121.8 0.3 slice.160
  122.2 3.8 collective-permute-done.8
  126.0 6.6 %collective-permute-done.9 = f32[8,8,8,1]{3,1,2,0:T(8,128)S(1)} collective-permute-done((f32[8,8,8,1]{3,1,2,0:T(8,128)S(1)}, f32[8,8,8,1]{3,1,2,0:T(8,128)S(1)}, u32[]{:S(2)}, u32[]{:S(2)}) %collective-permute-start.9) | collective-permute-done | bytes 2080 | tf_op jit(solution)/shard_map/ppermute | solution.py:25
  132.5 1.1 broadcast_multiply_fusion.6
  133.6 4.2 collective-permute-start.12
  137.9 0.2 broadcast_multiply_fusion.4
  138.1 0.3 slice.168
  138.6 5.9 %collective-permute-start.15 = (f32[8,8,1,512]{3,1,2,0:T(8,128)S(1)}, f32[8,8,1,512]{3,1,2,0:T(8,128)S(1)}, u32[]{:S(2)}, u32[]{:S(2)}) collective-permute-start(f32[8,8,1,512]{3,1,2,0:T(8,128)S(1)} %slice.174), channel_id=1, source_target_pairs={{0,2},{2,4},{4,6},{6,8},{8,10},{10,12},{12,14},{14,16},{16,18},{18... | collective-permute-start | bytes 393224 | tf_op jit(solution)/shard_map/ppermute | solution.py:31
  144.5 1.3 collective-permute-start.14
  145.8 0.1 slice.170
  146.0 3.7 collective-permute-start.13
  149.7 0.2 pad_maximum_fusion.12
  149.8 7.5 %collective-permute-done.13 = f32[8,8,8,1]{3,1,2,0:T(8,128)S(1)} collective-permute-done((f32[8,8,8,1]{3,1,2,0:T(8,128)S(1)}, f32[8,8,8,1]{3,1,2,0:T(8,128)S(1)}, u32[]{:S(2)}, u32[]{:S(2)}) %collective-permute-start.13) | collective-permute-done | bytes 2080 | tf_op jit(solution)/shard_map/ppermute | solution.py:25
  157.3 0.3 pad_maximum_fusion.13
  157.7 0.1 pad_maximum_fusion.15
  157.8 9.1 %collective-permute-done.14 = f32[8,8,1,512]{3,1,2,0:T(8,128)S(1)} collective-permute-done((f32[8,8,1,512]{3,1,2,0:T(8,128)S(1)}, f32[8,8,1,512]{3,1,2,0:T(8,128)S(1)}, u32[]{:S(2)}, u32[]{:S(2)}) %collective-permute-start.14) | collective-permute-done | bytes 131104 | tf_op jit(solution)/shard_map/ppermute | solution.py:31
  167.0 1.1 multiply_reduce_fusion
  168.1 0.7 copy.38
  168.8 66.4 %all-reduce.2.cloned.1.call-done = f32[8,8,512]{2,1,0:T(8,128)} async-done(((f32[8,8,512]{2,1,0:T(8,128)}), f32[8,8,512]{2,1,0:T(8,128)}) %all-reduce.2.cloned.1.call-update) | async-done | bytes 131088 | tf_op jit(solution)/shard_map/psum | solution.py:124
  235.3 1.7 multiply_reduce_fusion.1
  237.0 9.7 %psum.30 = f32[8]{0:T(128)S(1)} all-reduce(f32[8]{0:T(128)S(1)} %get-tuple-element.33), channel_id=1, replica_groups=mesh['face'=4,'tile'=64,'lev'=2] {'face'}, use_global_device_ids=true, to_apply=%region_6.7 | all-reduce | flops 8 | bytes 64 | tf_op jit(solution)/shard_map/psum | solution.py:128
  246.7 224.8 %psum.31 = f32[8]{0:T(128)S(1)} all-reduce(f32[8]{0:T(128)S(1)} %psum.30), channel_id=1, replica_groups=mesh['face'=4,'tile'=64,'lev'=2] {'tile'}, use_global_device_ids=true, to_apply=%region_7.8 | all-reduce | flops 8 | bytes 64 | tf_op jit(solution)/shard_map/psum | solution.py:128
  471.5 0.5 divide_subtract_fusion
  (47 shorter events, 0.7 us)
Async XLA Ops:
  7.2 23.8 %copy-start = (f32[2,8,8,512]{3,2,1,0:T(8,128)S(1)}, f32[2,8,8,512]{3,2,1,0:T(8,128)}, u32[]{:S(2)}) copy-start(f32[2,8,8,512]{3,2,1,0:T(8,128)} %param.13) | copy-start | bytes 786436
  7.2 23.8 %copy-start.1 = (s32[2,8,8,512]{3,2,1,0:T(8,128)S(1)}, s32[2,8,8,512]{3,2,1,0:T(8,128)}, u32[]{:S(2)}) copy-start(s32[2,8,8,512]{3,2,1,0:T(8,128)} %param.14) | copy-start | bytes 786436
  10.6 40.5 %all-to-all-start = ((f32[64,1,512]{2,1,0:T(1,128)}), f32[64,1,512]{2,1,0:T(1,128)S(1)}, u32[]{:S(2)}, u32[]{:S(2)}) async-start(f32[64,1,512]{2,1,0:T(1,128)} %reshape.69), calls=%async_computation | async-start | bytes 262144 | tf_op jit(solution)/shard_map/all_to_all | solution.py:93
  30.9 204.3 %all-reduce.2.cloned.1.call-start = ((), (), s32[]{:S(2)}) async-start(), calls=%async_computation.1 | async-start | bytes 262144 | tf_op jit(solution)/shard_map/psum | solution.py:124
  56.1 2.8 copy-start.4
  59.3 22.6 %collective-permute-start.2 = (f32[8,8,1,512]{3,1,2,0:T(8,128)S(1)}, f32[8,8,1,512]{3,1,2,0:T(8,128)S(1)}, u32[]{:S(2)}, u32[]{:S(2)}) collective-permute-start(f32[8,8,1,512]{3,1,2,0:T(8,128)S(1)} %get-tuple-element.25), channel_id=1, source_target_pairs={{0,2},{2,4},{4,6},{6,8},{8,10},{10,12},{12,14},{14,16},{16,18},{18... | collective-permute-start | bytes 393224 | tf_op jit(solution)/shard_map/ppermute | solution.py:17
  61.8 20.1 %collective-permute-start.3 = (f32[8,8,1,512]{3,1,2,0:T(8,128)S(1)}, f32[8,8,1,512]{3,1,2,0:T(8,128)S(1)}, u32[]{:S(2)}, u32[]{:S(2)}) collective-permute-start(f32[8,8,1,512]{3,1,2,0:T(8,128)S(1)} %get-tuple-element.26), channel_id=1, source_target_pairs={{2,0},{4,2},{6,4},{8,6},{10,8},{12,10},{14,12},{16,14},{18,16},{20... | collective-permute-start | bytes 393224 | tf_op jit(solution)/shard_map/ppermute | solution.py:18
  63.1 11.1 %collective-permute-start = (f32[8,8,8,1]{3,1,2,0:T(8,128)S(1)}, f32[8,8,8,1]{3,1,2,0:T(8,128)S(1)}, u32[]{:S(2)}, u32[]{:S(2)}) collective-permute-start(f32[8,8,8,1]{3,1,2,0:T(8,128)S(1)} %get-tuple-element.23), channel_id=1, source_target_pairs={{0,128},{128,256},{256,384},{384,0},{1,129},{129,257},{257,385},{3... | collective-permute-start | bytes 6152 | tf_op jit(solution)/shard_map/ppermute | solution.py:17
  66.1 15.9 %collective-permute-start.1 = (f32[8,8,8,1]{3,1,2,0:T(8,128)S(1)}, f32[8,8,8,1]{3,1,2,0:T(8,128)S(1)}, u32[]{:S(2)}, u32[]{:S(2)}) collective-permute-start(f32[8,8,8,1]{3,1,2,0:T(8,128)S(1)} %get-tuple-element.24), channel_id=1, source_target_pairs={{128,0},{256,128},{384,256},{0,384},{129,1},{257,129},{385,257},{1... | collective-permute-start | bytes 6152 | tf_op jit(solution)/shard_map/ppermute | solution.py:18
  82.7 17.8 %collective-permute-start.6 = (f32[8,8,1,512]{3,1,2,0:T(8,128)S(1)}, f32[8,8,1,512]{3,1,2,0:T(8,128)S(1)}, u32[]{:S(2)}, u32[]{:S(2)}) collective-permute-start(f32[8,8,1,512]{3,1,2,0:T(8,128)S(1)} %get-tuple-element.21), channel_id=1, source_target_pairs={{0,2},{2,4},{4,6},{6,8},{8,10},{10,12},{12,14},{14,16},{16,18},{18... | collective-permute-start | bytes 393224 | tf_op jit(solution)/shard_map/ppermute | solution.py:17
  84.0 17.3 %copy-start.2 = (f32[8,1,1,128]{3,2,1,0:T(1,128)S(1)}, f32[8,1,1,128]{3,2,1,0:T(1,128)}, u32[]{:S(2)}) copy-start(f32[8,1,1,128]{3,2,1,0:T(1,128)} %param.18) | copy-start | bytes 12292
  84.0 17.3 %copy-start.8 = (s32[1,1,128]{2,1,0:T(1,128)S(1)}, s32[1,1,128]{2,1,0:T(1,128)}, u32[]{:S(2)}) copy-start(s32[1,1,128]{2,1,0:T(1,128)} %param.15) | copy-start | bytes 1540
  84.0 16.5 %collective-permute-start.7 = (f32[8,8,1,512]{3,1,2,0:T(8,128)S(1)}, f32[8,8,1,512]{3,1,2,0:T(8,128)S(1)}, u32[]{:S(2)}, u32[]{:S(2)}) collective-permute-start(f32[8,8,1,512]{3,1,2,0:T(8,128)S(1)} %get-tuple-element.22), channel_id=1, source_target_pairs={{2,0},{4,2},{6,4},{8,6},{10,8},{12,10},{14,12},{16,14},{18,16},{20... | collective-permute-start | bytes 393224 | tf_op jit(solution)/shard_map/ppermute | solution.py:18
  85.5 15.0 %collective-permute-start.4 = (f32[8,8,8,1]{3,1,2,0:T(8,128)S(1)}, f32[8,8,8,1]{3,1,2,0:T(8,128)S(1)}, u32[]{:S(2)}, u32[]{:S(2)}) collective-permute-start(f32[8,8,8,1]{3,1,2,0:T(8,128)S(1)} %get-tuple-element.19), channel_id=1, source_target_pairs={{0,128},{128,256},{256,384},{384,0},{1,129},{129,257},{257,385},{3... | collective-permute-start | bytes 6152 | tf_op jit(solution)/shard_map/ppermute | solution.py:17
  91.0 9.6 %collective-permute-start.5 = (f32[8,8,8,1]{3,1,2,0:T(8,128)S(1)}, f32[8,8,8,1]{3,1,2,0:T(8,128)S(1)}, u32[]{:S(2)}, u32[]{:S(2)}) collective-permute-start(f32[8,8,8,1]{3,1,2,0:T(8,128)S(1)} %get-tuple-element.20), channel_id=1, source_target_pairs={{128,0},{256,128},{384,256},{0,384},{129,1},{257,129},{385,257},{1... | collective-permute-start | bytes 6152 | tf_op jit(solution)/shard_map/ppermute | solution.py:18
  92.9 10.9 %copy-start.3 = (f32[8,1,1,128]{3,2,1,0:T(1,128)S(1)}, f32[8,1,1,128]{3,2,1,0:T(1,128)}, u32[]{:S(2)}) copy-start(f32[8,1,1,128]{3,2,1,0:T(1,128)} %param.17) | copy-start | bytes 12292
  92.9 13.5 %copy-start.6 = (f32[1,1,128]{2,1,0:T(1,128)S(1)}, f32[1,1,128]{2,1,0:T(1,128)}, u32[]{:S(2)}) copy-start(f32[1,1,128]{2,1,0:T(1,128)} %param.19) | copy-start | bytes 1540
  92.9 13.5 %copy-start.7 = (f32[1,1,128]{2,1,0:T(1,128)S(1)}, f32[1,1,128]{2,1,0:T(1,128)}, u32[]{:S(2)}) copy-start(f32[1,1,128]{2,1,0:T(1,128)} %param.20) | copy-start | bytes 1540
  108.8 23.7 %collective-permute-start.10 = (f32[8,8,1,512]{3,1,2,0:T(8,128)S(1)}, f32[8,8,1,512]{3,1,2,0:T(8,128)S(1)}, u32[]{:S(2)}, u32[]{:S(2)}) collective-permute-start(f32[8,8,1,512]{3,1,2,0:T(8,128)S(1)} %slice.165), channel_id=1, source_target_pairs={{2,0},{4,2},{6,4},{8,6},{10,8},{12,10},{14,12},{16,14},{18,16},{20... | collective-permute-start | bytes 393224 | tf_op jit(solution)/shard_map/ppermute | solution.py:31
  110.1 22.4 %collective-permute-start.11 = (f32[8,8,1,512]{3,1,2,0:T(8,128)S(1)}, f32[8,8,1,512]{3,1,2,0:T(8,128)S(1)}, u32[]{:S(2)}, u32[]{:S(2)}) collective-permute-start(f32[8,8,1,512]{3,1,2,0:T(8,128)S(1)} %slice.166), channel_id=1, source_target_pairs={{0,2},{2,4},{4,6},{6,8},{8,10},{10,12},{12,14},{14,16},{16,18},{18... | collective-permute-start | bytes 393224 | tf_op jit(solution)/shard_map/ppermute | solution.py:31
  115.2 10.7 %collective-permute-start.8 = (f32[8,8,8,1]{3,1,2,0:T(8,128)S(1)}, f32[8,8,8,1]{3,1,2,0:T(8,128)S(1)}, u32[]{:S(2)}, u32[]{:S(2)}) collective-permute-start(f32[8,8,8,1]{3,1,2,0:T(8,128)S(1)} %slice.161), channel_id=1, source_target_pairs={{0,384},{128,0},{256,128},{384,256},{1,385},{129,1},{257,129},{385... | collective-permute-start | bytes 6152 | tf_op jit(solution)/shard_map/ppermute | solution.py:25
  118.4 14.1 %collective-permute-start.9 = (f32[8,8,8,1]{3,1,2,0:T(8,128)S(1)}, f32[8,8,8,1]{3,1,2,0:T(8,128)S(1)}, u32[]{:S(2)}, u32[]{:S(2)}) collective-permute-start(f32[8,8,8,1]{3,1,2,0:T(8,128)S(1)} %slice.162), channel_id=1, source_target_pairs={{0,128},{128,256},{256,384},{384,0},{1,129},{129,257},{257,385},{3... | collective-permute-start | bytes 6152 | tf_op jit(solution)/shard_map/ppermute | solution.py:25
  133.6 16.0 %collective-permute-start.12 = (f32[8,8,8,1]{3,1,2,0:T(8,128)S(1)}, f32[8,8,8,1]{3,1,2,0:T(8,128)S(1)}, u32[]{:S(2)}, u32[]{:S(2)}) collective-permute-start(f32[8,8,8,1]{3,1,2,0:T(8,128)S(1)} %slice.169), channel_id=1, source_target_pairs={{0,384},{128,0},{256,128},{384,256},{1,385},{129,1},{257,129},{385... | collective-permute-start | bytes 6152 | tf_op jit(solution)/shard_map/ppermute | solution.py:25
  138.6 19.1 %collective-permute-start.15 = (f32[8,8,1,512]{3,1,2,0:T(8,128)S(1)}, f32[8,8,1,512]{3,1,2,0:T(8,128)S(1)}, u32[]{:S(2)}, u32[]{:S(2)}) collective-permute-start(f32[8,8,1,512]{3,1,2,0:T(8,128)S(1)} %slice.174), channel_id=1, source_target_pairs={{0,2},{2,4},{4,6},{6,8},{8,10},{10,12},{12,14},{14,16},{16,18},{18... | collective-permute-start | bytes 393224 | tf_op jit(solution)/shard_map/ppermute | solution.py:31
  144.5 22.3 %collective-permute-start.14 = (f32[8,8,1,512]{3,1,2,0:T(8,128)S(1)}, f32[8,8,1,512]{3,1,2,0:T(8,128)S(1)}, u32[]{:S(2)}, u32[]{:S(2)}) collective-permute-start(f32[8,8,1,512]{3,1,2,0:T(8,128)S(1)} %slice.173), channel_id=1, source_target_pairs={{2,0},{4,2},{6,4},{8,6},{10,8},{12,10},{14,12},{16,14},{18,16},{20... | collective-permute-start | bytes 393224 | tf_op jit(solution)/shard_map/ppermute | solution.py:31
  146.0 11.4 %collective-permute-start.13 = (f32[8,8,8,1]{3,1,2,0:T(8,128)S(1)}, f32[8,8,8,1]{3,1,2,0:T(8,128)S(1)}, u32[]{:S(2)}, u32[]{:S(2)}) collective-permute-start(f32[8,8,8,1]{3,1,2,0:T(8,128)S(1)} %slice.170), channel_id=1, source_target_pairs={{0,128},{128,256},{256,384},{384,0},{1,129},{129,257},{257,385},{3... | collective-permute-start | bytes 6152 | tf_op jit(solution)/shard_map/ppermute | solution.py:25
  166.9 68.3 %copy-start.5 = (f32[8]{0:T(128)S(1)}, f32[8]{0:T(128)}, u32[]{:S(2)}) copy-start(f32[8]{0:T(128)} %param.21) | copy-start | bytes 100
Sparse Core Ops, SparseCore 0:
  169.0 66.2 all-reduce.1
